TPU v7x, 512 devices: a whole 4x4x16 slice. The times are simulated.
512 devices in a mesh: half: 2 (over core), row: 16 (over z), col: 16 (over y, x).
Axes of the slice: x: 4, y: 4, z: 16, core: 2. Of those that a mesh axis runs over, the one named last changes fastest.
Arguments:
- child_front: float32 [2, 8192, 8192], P('half', 'row', 'col'), as said below
- child_map: int32 [2, 48], P('half'), may hold values from 0 to 63, as said below
- root_front: float32 [8192, 16, 2, 256], P('row', 'col', 'half'), as said below
Outputs:
- child_panel: float32 [2, 512, 8192], P('half', None, 'col')
- root_panel: float32 [512, 16, 2, 256], P(None, 'col', 'half')
- root_update: float32 [8192, 16, 2, 256], P('row', 'col', 'half')
Inputs may be any that keep to these rules, and one draw needn't show every extreme that they name: `child_map`: for child h, the update blocks of row part k (the 3 blocks after that part's first block) map in increasing order to distinct blocks among the root's blocks k * 4 to (k + 1) * 4 - 1. `child_front`: each child's front is symmetric and positive definite. `root_front`: the root front is symmetric and positive definite.
All inputs are finite; a program needn't handle non-finite values.
Results may differ from a plain program's by a relative error of at most 0.0001.
Values sent between devices are 32-bit elements; how exact they have to be, the bound alone decides.
A program may use at most 64 MiB of HBM per device.

v0:
```python
import jax
import jax.numpy as jnp
from jax import lax
from jax.sharding import PartitionSpec as P

BLK = 128
PB = 32


def spread_2(value, axis, source):
    kept = jnp.where(lax.axis_index(axis) == source, value, 0).astype(value.dtype)
    return lax.psum(kept, axis)


def lower_solve(factor, right):
    return lax.linalg.triangular_solve(factor, right, left_side=True, lower=True)


def transposed_product(left, right):
    return lax.dot_general(
        left,
        right,
        (((0,), (0,)), ((), ())),
        precision=lax.Precision.HIGHEST,
        preferred_element_type=jnp.float32,
    )


def selector(child_row_map, part_index, child_tiles, root_tiles):
    per_part = child_tiles - 1
    targets = (
        lax.dynamic_slice_in_dim(child_row_map, part_index * per_part, per_part)
        - part_index * root_tiles
    )
    one_hot = (jnp.arange(root_tiles, dtype=jnp.int32)[:, None] == targets[None, :]).astype(
        jnp.float32
    )
    return jnp.concatenate([jnp.zeros((root_tiles, 1), jnp.float32), one_hot], axis=1)


def body(child_front, child_map, root_front):
    tile_rows = BLK
    pivot_count = PB
    child_block = child_front[0]
    part_rows = child_block.shape[0]
    row_part = lax.axis_index("row")
    col_part = lax.axis_index("col")
    strips = lax.all_gather(child_block[:pivot_count, :], "row", axis=0, tiled=True)
    pieces = lax.all_gather(
        child_block[None, :pivot_count, :pivot_count], ("row", "col"), axis=0, tiled=True
    )
    parts_count = lax.axis_size("row")
    corner = pieces.reshape(parts_count, parts_count, pivot_count, pivot_count).transpose(
        0, 2, 1, 3
    )
    corner = corner.reshape(parts_count * pivot_count, parts_count * pivot_count)
    factor = jnp.linalg.cholesky(corner)
    child_panel = lower_solve(factor, strips)
    columns = lax.all_gather(child_block[:, :pivot_count], "col", axis=1, tiled=True)
    panel_rows = lower_solve(factor, columns.T)
    update = child_block - transposed_product(panel_rows, child_panel)
    root_rows = root_front.shape[0]
    child_tiles = part_rows // tile_rows
    root_tiles = root_rows // tile_rows
    own_map = child_map[0]
    row_select = selector(own_map, row_part, child_tiles, root_tiles)
    col_select = selector(own_map, col_part, child_tiles, root_tiles)
    blocks = update.reshape(child_tiles, tile_rows, child_tiles, tile_rows)
    spread = jnp.einsum("ap,piqj->aiqj", row_select, blocks, precision=lax.Precision.HIGHEST)
    spread = jnp.einsum("aiqj,bq->aibj", spread, col_select, precision=lax.Precision.HIGHEST)
    additions = spread.reshape(root_rows, 2, root_rows // 2)
    joined = lax.psum_scatter(additions, "half", scatter_dimension=1, tiled=True)
    assembled = root_front[:, 0, 0, :] + joined[:, 0, :]
    root_strips = lax.all_gather(assembled[:pivot_count, :], "row", axis=0, tiled=True)
    pivots = spread_2(root_strips[:, :pivot_count], "half", 0)
    root_corner = lax.all_gather(pivots, "col", axis=1, tiled=True)
    root_factor = jnp.linalg.cholesky(root_corner)
    root_panel = lower_solve(root_factor, root_strips)
    mirrored = spread_2(root_panel, "col", row_part)
    both_halves = lax.all_gather(mirrored[:, None, :], "half", axis=1, tiled=True)
    panel_side = both_halves.reshape(both_halves.shape[0], root_rows)
    root_update = assembled - transposed_product(panel_side, root_panel)
    return (child_panel[None], root_panel[:, None, None, :], root_update[:, None, None, :])


def solution(mesh):
    return jax.shard_map(
        body,
        mesh=mesh,
        in_specs=(P("half", "row", "col"), P("half", None), P("row", "col", "half", None)),
        out_specs=(
            P("half", None, "col"),
            P(None, "col", "half", None),
            P("row", "col", "half", None),
        ),
        check_vma=False,
    )
```

profile of v0, /device:TPU:1, one launch (start us, length us, event | category | flops | bytes accessed | tf_op | source)
XLA Modules:
  0.0 844.2 jit_solution(4435899986150828886)
XLA Ops:
  12.8 208.7 %all-gather.14.cloned.1.call-done = f32[8192,32]{1,0:T(8,128)} async-done(((f32[32,32]{1,0:T(8,128)}), f32[8192,32]{1,0:T(8,128)}) %all-gather.14.cloned.1.call-update) | async-done | bytes 1048592 | tf_op jit(solution)/shard_map/all_gather | solution.py:49
  221.5 5.6 copy.23
  227.1 3.5 reshape.68
  232.2 11.7 %cholesky.286 = f32[128,128]{1,0:T(8,128)S(1)} custom-call(f32[128,128]{1,0:T(8,128)S(1)} %cholesky.426), custom_call_target="Cholesky" | custom-call | tf_op jit(solution)/shard_map/jit(cholesky)/cholesky | solution.py:57
  244.0 9.8 %custom-call.31 = f32[1,128,128]{1,2,0:T(8,128)S(1)} custom-call(f32[1,128,128]{2,1,0:T(8,128)S(1)} %get-tuple-element.79), custom_call_target="InvertDiagBlocksLowerTriangular" | custom-call | tf_op jit(solution)/shard_map/jit(cholesky)/cholesky | solution.py:57
  256.4 11.7 %cholesky.305 = f32[128,128]{1,0:T(8,128)S(1)} custom-call(f32[128,128]{1,0:T(8,128)S(1)} %cholesky.430), custom_call_target="Cholesky" | custom-call | tf_op jit(solution)/shard_map/jit(cholesky)/cholesky | solution.py:57
  268.2 10.0 %custom-call.32 = f32[1,128,128]{1,2,0:T(8,128)S(1)} custom-call(f32[1,128,128]{2,1,0:T(8,128)S(1)} %get-tuple-element.76), custom_call_target="InvertDiagBlocksLowerTriangular" | custom-call | tf_op jit(solution)/shard_map/jit(cholesky)/cholesky | solution.py:57
  279.7 11.7 %cholesky.326 = f32[128,128]{1,0:T(8,128)S(1)} custom-call(f32[128,128]{1,0:T(8,128)S(1)} %cholesky.435), custom_call_target="Cholesky" | custom-call | tf_op jit(solution)/shard_map/jit(cholesky)/cholesky | solution.py:57
  292.2 9.8 %custom-call.33 = f32[1,128,128]{1,2,0:T(8,128)S(1)} custom-call(f32[1,128,128]{2,1,0:T(8,128)S(1)} %get-tuple-element.73), custom_call_target="InvertDiagBlocksLowerTriangular" | custom-call | tf_op jit(solution)/shard_map/jit(cholesky)/cholesky | solution.py:57
  303.5 11.7 %cholesky.343 = f32[128,128]{1,0:T(8,128)S(1)} custom-call(f32[128,128]{1,0:T(8,128)S(1)} %convolution_subtract_fusion.16), custom_call_target="Cholesky" | custom-call | tf_op jit(solution)/shard_map/jit(cholesky)/cholesky | solution.py:57
  319.6 8.5 %while.6 = (s32[]{:T(128)}, f32[512,512]{1,0:T(8,128)S(1)}, s32[4,2]{0,1:T(2,128)S(1)}, f32[4,128,128]{2,1,0:T(8,128)S(1)}, s32[]{:T(128)}) while((s32[]{:T(128)}, f32[512,512]{1,0:T(8,128)S(1)}, s32[4,2]{0,1:T(2,128)S(1)}, f32[4,128,128]{2,1,0:T(8,128)S(1)}, s32[]{:T(128)}) %tuple.64), condition=%wide.while_cond, body=%wide.while_body.sunk | while | flops 2 | bytes 131181 | solution.py:16
  328.1 39.3 %custom-call.34 = f32[4,128,128]{1,2,0:T(8,128)S(1)} custom-call(f32[4,128,128]{2,1,0:T(8,128)S(1)} %get-tuple-element.27), custom_call_target="InvertDiagBlocksLowerTriangular" | custom-call | tf_op jit(solution)/shard_map/triangular_solve/custom-call.3 | solution.py:16
  373.1 1.6 convolution_subtract_fusion.6
  380.8 1.6 convolution_subtract_fusion.7
  383.6 3.1 convolution_subtract_fusion
  387.0 1.7 fusion.11
  392.0 23.3 %reduce-scatter.2.cloned.1.call-done = f32[512,1,256]{2,0,1:T(8,128)} async-done(((f32[512,2,256]{2,0,1:T(8,128)}), f32[512,1,256]{2,0,1:T(8,128)}) %reduce-scatter.2.cloned.1.call-update) | async-done | bytes 524304 | tf_op jit(solution)/shard_map/reduce_scatter | solution.py:72
  417.2 25.4 %all_gather.21 = f32[512,256]{1,0:T(8,128)S(1)} all-gather(f32[32,256]{1,0:T(8,128)S(1)} %slice.211), channel_id=1, replica_groups=mesh['half'=2,'row'=16,'col'=16] {'row'}, dimensions={0}, use_global_device_ids=true | all-gather | bytes 557056 | tf_op jit(solution)/shard_map/all_gather | solution.py:74
  443.4 44.3 %all-reduce.6.cloned.1.call-done = f32[512,32]{0,1:T(8,128)} async-done(((f32[512,32]{0,1:T(8,128)}), f32[512,32]{0,1:T(8,128)}) %all-reduce.6.cloned.1.call-update) | async-done | bytes 65552 | tf_op jit(solution)/shard_map/psum | solution.py:12
  487.9 59.6 %all-gather.10.cloned.1.call-done = f32[512,512]{0,1:T(8,128)} async-done(((f32[512,32]{0,1:T(8,128)}), f32[512,512]{0,1:T(8,128)}) %all-gather.10.cloned.1.call-update) | async-done | bytes 1048592 | tf_op jit(solution)/shard_map/all_gather | solution.py:76
  550.5 11.7 %cholesky.358 = f32[128,128]{1,0:T(8,128)S(1)} custom-call(f32[128,128]{1,0:T(8,128)S(1)} %cholesky.439), custom_call_target="Cholesky" | custom-call | tf_op jit(solution)/shard_map/jit(cholesky)/cholesky | solution.py:77
  562.4 9.8 %custom-call.36 = f32[1,128,128]{1,2,0:T(8,128)S(1)} custom-call(f32[1,128,128]{2,1,0:T(8,128)S(1)} %get-tuple-element.69), custom_call_target="InvertDiagBlocksLowerTriangular" | custom-call | tf_op jit(solution)/shard_map/jit(cholesky)/cholesky | solution.py:77
  573.6 11.7 %cholesky.377 = f32[128,128]{1,0:T(8,128)S(1)} custom-call(f32[128,128]{1,0:T(8,128)S(1)} %cholesky.443), custom_call_target="Cholesky" | custom-call | tf_op jit(solution)/shard_map/jit(cholesky)/cholesky | solution.py:77
  586.7 10.0 %custom-call.37 = f32[1,128,128]{1,2,0:T(8,128)S(1)} custom-call(f32[1,128,128]{2,1,0:T(8,128)S(1)} %get-tuple-element.66), custom_call_target="InvertDiagBlocksLowerTriangular" | custom-call | tf_op jit(solution)/shard_map/jit(cholesky)/cholesky | solution.py:77
  598.8 13.2 %cholesky.398 = f32[128,128]{1,0:T(8,128)} custom-call(f32[128,128]{1,0:T(8,128)} %cholesky.448), custom_call_target="Cholesky" | custom-call | tf_op jit(solution)/shard_map/jit(cholesky)/cholesky | solution.py:77
  614.2 11.3 %custom-call.38 = f32[1,128,128]{1,2,0:T(8,128)} custom-call(f32[1,128,128]{2,1,0:T(8,128)} %get-tuple-element.63), custom_call_target="InvertDiagBlocksLowerTriangular" | custom-call | tf_op jit(solution)/shard_map/jit(cholesky)/cholesky | solution.py:77
  626.9 11.7 %cholesky.415 = f32[128,128]{1,0:T(8,128)S(1)} custom-call(f32[128,128]{1,0:T(8,128)S(1)} %convolution_subtract_fusion.15), custom_call_target="Cholesky" | custom-call | tf_op jit(solution)/shard_map/jit(cholesky)/cholesky | solution.py:77
  642.2 8.0 while.5
  650.2 39.3 %custom-call.26 = f32[4,128,128]{1,2,0:T(8,128)S(1)} custom-call(f32[4,128,128]{2,1,0:T(8,128)S(1)} %get-tuple-element.20), custom_call_target="InvertDiagBlocksLowerTriangular" | custom-call | tf_op jit(solution)/shard_map/triangular_solve | solution.py:16
  693.7 115.5 %all-reduce.8.cloned.1.call-done = f32[512,1,256]{2,0,1:T(8,128)} async-done(((f32[512,1,256]{2,0,1:T(8,128)}), f32[512,1,256]{2,0,1:T(8,128)}) %all-reduce.8.cloned.1.call-update) | async-done | bytes 524304 | tf_op jit(solution)/shard_map/psum | solution.py:12
  809.2 2.0 fusion.23
  812.5 20.5 %all-gather.12.cloned.1.call-done = f32[512,2,256]{2,0,1:T(8,128)} async-done(((f32[512,1,256]{2,0,1:T(8,128)}), f32[512,2,256]{2,0,1:T(8,128)}) %all-gather.12.cloned.1.call-update) | async-done | bytes 1048592 | tf_op jit(solution)/shard_map/all_gather | solution.py:80
  (146 shorter events, 73.0 us)
Async XLA Ops:
  7.2 214.4 %all-gather.14.cloned.1.call-start = ((), (), s32[]{:S(2)}) async-start(), calls=%async_computation.7 | async-start | bytes 4210688 | tf_op jit(solution)/shard_map/all_gather | solution.py:49
  8.6 358.9 %all-gather.8.cloned.1.call-start = ((), (), s32[]{:S(2)}) async-start(), calls=%async_computation.1 | async-start | bytes 1114112 | tf_op jit(solution)/shard_map/all_gather | solution.py:59
  10.3 365.5 %all-gather.16.cloned.1.call-start = ((), (), s32[]{:S(2)}) async-start(), calls=%async_computation.8 | async-start | bytes 1114112 | tf_op jit(solution)/shard_map/all_gather | solution.py:48
  11.9 403.3 %reduce-scatter.2.cloned.1.call-start = ((), (), s32[]{:S(2)}) async-start(), calls=%async_computation.2 | async-start | bytes 1572864 | tf_op jit(solution)/shard_map/reduce_scatter | solution.py:72
  231.2 1.0 copy-start
  372.4 0.7 copy-start.3
  375.8 7.7 copy-start.4
  375.8 7.7 copy-start.9
  382.9 0.7 copy-start.5
  388.7 26.5 %copy-start.7 = (f32[512,1,1,256]{3,2,1,0:T(1,128)S(1)}, f32[512,1,1,256]{3,2,1,0:T(1,128)}, u32[]{:S(2)}) copy-start(f32[512,1,1,256]{3,2,1,0:T(1,128)} %param.8) | copy-start | bytes 1572868
  391.9 95.8 %all-reduce.6.cloned.1.call-start = ((), (), s32[]{:S(2)}) async-start(), calls=%async_computation.3 | async-start | bytes 131072 | tf_op jit(solution)/shard_map/psum | solution.py:12
  416.4 0.8 copy-start.1
  443.3 104.2 %all-gather.10.cloned.1.call-start = ((), (), s32[]{:S(2)}) async-start(), calls=%async_computation.4 | async-start | bytes 1114112 | tf_op jit(solution)/shard_map/all_gather | solution.py:76
  487.7 321.4 %all-reduce.8.cloned.1.call-start = ((), (), s32[]{:S(2)}) async-start(), calls=%async_computation.5 | async-start | bytes 1048576 | tf_op jit(solution)/shard_map/psum | solution.py:12
  572.9 0.7 copy-start.6
  689.6 1.5 copy-start.8
  691.5 143.1 %copy-start.2 = (f32[512,256]{1,0:T(8,128)S(1)}, f32[512,256]{1,0:T(8,128)}, u32[]{:S(2)}) copy-start(f32[512,256]{1,0:T(8,128)} %copy-done.1) | copy-start | bytes 1572868
  693.6 139.4 %all-gather.12.cloned.1.call-start = ((), (), s32[]{:S(2)}) async-start(), calls=%async_computation.6 | async-start | bytes 1572864 | tf_op jit(solution)/shard_map/all_gather | solution.py:80
Sparse Core Ops, SparseCore 0:
  13.1 208.4 all-gather.13
  225.1 59.4 all-gather.7
  287.2 63.2 all-gather.15
  392.0 23.1 reduce-scatter.1
  443.5 44.1 all-reduce.5
  491.0 56.4 all-gather.9
  693.7 115.3 all-reduce.7
  811.2 21.7 all-gather.11
where the time goes:
time: 855 us; the launch traced here: 844 us
  waiting for transfers between devices  472 us (55%)
  other arithmetic  248 us (29%)
  local copies, waits for them, and re-layouts  43.7 us (5%)
  matrix products  33.6 us (4%)
  blocking collectives  25.4 us (3%)
  between operations  20.3 us (2%)
    all_gather x1, waiting for transfers between devices, body(): lax.all_gather(child_block[None, :pivot_count, :pivot_count], ('row', 'co...  209 us
    psum x2, waiting for transfers between devices, spread_2(): return lax.psum(kept, axis)  160 us
    another operation x15, other arithmetic, body(): root_factor = jnp.linalg.cholesky(root_corner)  83.6 us
    another operation x5, other arithmetic, lower_solve(): lax.linalg.triangular_solve(factor, right, left_side=True, lower=True)  79.1 us
    another operation x14, other arithmetic, body(): factor = jnp.linalg.cholesky(corner)  78.6 us
    all_gather x1, waiting for transfers between devices, body(): root_corner = lax.all_gather(pivots, 'col', axis=1, tiled=True)  59.6 us
    all_gather x1, blocking collectives, body(): lax.all_gather(assembled[:pivot_count, :], 'row', axis=0, tiled=True)  25.4 us
    reduce_scatter x1, waiting for transfers between devices, body(): lax.psum_scatter(additions, 'half', scatter_dimension=1, tiled=True)  23.3 us
  transfers between devices with their start and end apart: 8, of which 6 were waited for; matrix products, arithmetic and copies ran while one was open for 19% of the time, Pallas kernels for 0%

commit v1 on v0

--- a/solution.py
+++ b/solution.py
@@ -2,6 +2,7 @@
 import jax.numpy as jnp
 from jax import lax
 from jax.sharding import PartitionSpec as P
+from jax.lax import all_to_all, psum
 
 BLK = 128
 PB = 32
@@ -73,7 +74,10 @@
     assembled = root_front[:, 0, 0, :] + joined[:, 0, :]
     root_strips = lax.all_gather(assembled[:pivot_count, :], "row", axis=0, tiled=True)
     pivots = spread_2(root_strips[:, :pivot_count], "half", 0)
-    root_corner = lax.all_gather(pivots, "col", axis=1, tiled=True)
+    sides = psum(1, "col")
+    queue = [sides if at == 1 else 1 for at in range(pivots.ndim)]
+    state_next = jnp.tile(pivots, queue)
+    root_corner = all_to_all(state_next, "col", split_axis=1, concat_axis=1, tiled=True)
     root_factor = jnp.linalg.cholesky(root_corner)
     root_panel = lower_solve(root_factor, root_strips)
     mirrored = spread_2(root_panel, "col", row_part)

time: 855 us -> 813 us (0.951)
  waiting for transfers between devices: 472 us -> 428 us
    all_gather x1 -> x0, waiting for transfers between devices: 59.6 us -> none  [body(): root_corner = lax.all_gather(pivots, 'col', axis=1, tiled=True)]
    all_to_all x0 -> x1, waiting for transfers between devices: none -> 16.3 us  [body(): all_to_all(state_next, 'col', split_axis=1, concat_axis=1, tiled=True)]
  transfers between devices with their start and end apart: 8 -> 8, of which waited for: 6 -> 6; matrix products, arithmetic and copies ran while one was open for 19% -> 20% of each run, Pallas kernels for 0% -> 0%
where the time goes in v1:
time: 813 us; the launch traced here: 802 us
  waiting for transfers between devices  428 us (53%)
  other arithmetic  243 us (30%)
  local copies, waits for them, and re-layouts  43.8 us (5%)
  matrix products  35.5 us (4%)
  blocking collectives  25.4 us (3%)
  between operations  20.3 us (2%)
    all_gather x1, waiting for transfers between devices, body(): lax.all_gather(child_block[None, :pivot_count, :pivot_count], ('row', 'co...  209 us
    psum x2, waiting for transfers between devices, spread_2(): return lax.psum(kept, axis)  159 us
    another operation x5, other arithmetic, lower_solve(): lax.linalg.triangular_solve(factor, right, left_side=True, lower=True)  79.5 us
    another operation x15, other arithmetic, body(): root_factor = jnp.linalg.cholesky(root_corner)  79.2 us
    another operation x14, other arithmetic, body(): factor = jnp.linalg.cholesky(corner)  78.6 us
    all_gather x1, blocking collectives, body(): lax.all_gather(assembled[:pivot_count, :], 'row', axis=0, tiled=True)  25.4 us
    reduce_scatter x1, waiting for transfers between devices, body(): lax.psum_scatter(additions, 'half', scatter_dimension=1, tiled=True)  23.3 us
    all_gather x1, waiting for transfers between devices, body(): lax.all_gather(mirrored[:, None, :], 'half', axis=1, tiled=True)  20.7 us
  transfers between devices with their start and end apart: 8, of which 6 were waited for; matrix products, arithmetic and copies ran while one was open for 20% of the time, Pallas kernels for 0%

profile of v1, /device:TPU:1, one launch (start us, length us, event | category | flops | bytes accessed | tf_op | source)
XLA Modules:
  0.0 802.4 jit_solution(15668333136225276405)
XLA Ops:
  12.8 208.7 %all-gather.11.cloned.1.call-done = f32[8192,32]{1,0:T(8,128)} async-done(((f32[32,32]{1,0:T(8,128)}), f32[8192,32]{1,0:T(8,128)}) %all-gather.11.cloned.1.call-update) | async-done | bytes 1048592 | tf_op jit(solution)/shard_map/all_gather | solution.py:50
  221.5 5.6 copy.21
  227.1 3.5 reshape.75
  232.2 11.7 %cholesky.286 = f32[128,128]{1,0:T(8,128)S(1)} custom-call(f32[128,128]{1,0:T(8,128)S(1)} %cholesky.426), custom_call_target="Cholesky" | custom-call | tf_op jit(solution)/shard_map/jit(cholesky)/cholesky | solution.py:58
  244.0 9.8 %custom-call.31 = f32[1,128,128]{1,2,0:T(8,128)S(1)} custom-call(f32[1,128,128]{2,1,0:T(8,128)S(1)} %get-tuple-element.79), custom_call_target="InvertDiagBlocksLowerTriangular" | custom-call | tf_op jit(solution)/shard_map/jit(cholesky)/cholesky | solution.py:58
  256.4 11.7 %cholesky.305 = f32[128,128]{1,0:T(8,128)S(1)} custom-call(f32[128,128]{1,0:T(8,128)S(1)} %cholesky.430), custom_call_target="Cholesky" | custom-call | tf_op jit(solution)/shard_map/jit(cholesky)/cholesky | solution.py:58
  268.2 10.0 %custom-call.32 = f32[1,128,128]{1,2,0:T(8,128)S(1)} custom-call(f32[1,128,128]{2,1,0:T(8,128)S(1)} %get-tuple-element.76), custom_call_target="InvertDiagBlocksLowerTriangular" | custom-call | tf_op jit(solution)/shard_map/jit(cholesky)/cholesky | solution.py:58
  279.7 11.7 %cholesky.326 = f32[128,128]{1,0:T(8,128)S(1)} custom-call(f32[128,128]{1,0:T(8,128)S(1)} %cholesky.435), custom_call_target="Cholesky" | custom-call | tf_op jit(solution)/shard_map/jit(cholesky)/cholesky | solution.py:58
  292.2 9.8 %custom-call.33 = f32[1,128,128]{1,2,0:T(8,128)S(1)} custom-call(f32[1,128,128]{2,1,0:T(8,128)S(1)} %get-tuple-element.73), custom_call_target="InvertDiagBlocksLowerTriangular" | custom-call | tf_op jit(solution)/shard_map/jit(cholesky)/cholesky | solution.py:58
  303.5 11.7 %cholesky.343 = f32[128,128]{1,0:T(8,128)S(1)} custom-call(f32[128,128]{1,0:T(8,128)S(1)} %convolution_subtract_fusion.16), custom_call_target="Cholesky" | custom-call | tf_op jit(solution)/shard_map/jit(cholesky)/cholesky | solution.py:58
  319.2 8.5 %while.6 = (s32[]{:T(128)}, f32[512,512]{1,0:T(8,128)S(1)}, s32[4,2]{0,1:T(2,128)S(1)}, f32[4,128,128]{2,1,0:T(8,128)S(1)}, s32[]{:T(128)}) while((s32[]{:T(128)}, f32[512,512]{1,0:T(8,128)S(1)}, s32[4,2]{0,1:T(2,128)S(1)}, f32[4,128,128]{2,1,0:T(8,128)S(1)}, s32[]{:T(128)}) %tuple.64), condition=%wide.while_cond, body=%wide.while_body.sunk | while | flops 2 | bytes 131181 | solution.py:17
  327.7 39.7 %custom-call.34 = f32[4,128,128]{1,2,0:T(8,128)S(1)} custom-call(f32[4,128,128]{2,1,0:T(8,128)S(1)} %get-tuple-element.27), custom_call_target="InvertDiagBlocksLowerTriangular" | custom-call | tf_op jit(solution)/shard_map/triangular_solve/custom-call.3 | solution.py:17
  380.8 1.6 convolution_subtract_fusion.7
  383.6 3.1 convolution_subtract_fusion
  387.0 1.7 fusion.11
  392.0 23.3 %reduce-scatter.2.cloned.1.call-done = f32[512,1,256]{2,0,1:T(8,128)} async-done(((f32[512,2,256]{2,0,1:T(8,128)}), f32[512,1,256]{2,0,1:T(8,128)}) %reduce-scatter.2.cloned.1.call-update) | async-done | bytes 524304 | tf_op jit(solution)/shard_map/reduce_scatter | solution.py:73
  417.2 25.4 %all_gather.18 = f32[512,256]{1,0:T(8,128)S(1)} all-gather(f32[32,256]{1,0:T(8,128)S(1)} %slice.211), channel_id=1, replica_groups=mesh['half'=2,'row'=16,'col'=16] {'row'}, dimensions={0}, use_global_device_ids=true | all-gather | bytes 557056 | tf_op jit(solution)/shard_map/all_gather | solution.py:75
  443.3 44.9 %all-reduce.6.cloned.1.call-done = f32[512,32]{1,0:T(8,128)} async-done(((f32[512,32]{1,0:T(8,128)}), f32[512,32]{1,0:T(8,128)}) %all-reduce.6.cloned.1.call-update) | async-done | bytes 65552 | tf_op jit(solution)/shard_map/psum | solution.py:13
  490.3 5.7 all-to-all-start
  496.1 16.3 %all-to-all-done = f32[512,16,32]{0,2,1:T(8,128)S(1)} async-done(((f32[512,16,32]{0,2,1:T(8,128)}), f32[512,16,32]{0,2,1:T(8,128)S(1)}, u32[]{:S(2)}, u32[]{:S(2)}) %all-to-all-start) | async-done | bytes 1048608 | tf_op jit(solution)/shard_map/all_to_all | solution.py:80
  514.0 11.7 %cholesky.358 = f32[128,128]{1,0:T(8,128)S(1)} custom-call(f32[128,128]{1,0:T(8,128)S(1)} %cholesky.439), custom_call_target="Cholesky" | custom-call | tf_op jit(solution)/shard_map/jit(cholesky)/cholesky | solution.py:81
  525.9 9.8 %custom-call.36 = f32[1,128,128]{1,2,0:T(8,128)S(1)} custom-call(f32[1,128,128]{2,1,0:T(8,128)S(1)} %get-tuple-element.69), custom_call_target="InvertDiagBlocksLowerTriangular" | custom-call | tf_op jit(solution)/shard_map/jit(cholesky)/cholesky | solution.py:81
  538.2 11.7 %cholesky.377 = f32[128,128]{1,0:T(8,128)S(1)} custom-call(f32[128,128]{1,0:T(8,128)S(1)} %cholesky.443), custom_call_target="Cholesky" | custom-call | tf_op jit(solution)/shard_map/jit(cholesky)/cholesky | solution.py:81
  551.3 10.0 %custom-call.37 = f32[1,128,128]{1,2,0:T(8,128)S(1)} custom-call(f32[1,128,128]{2,1,0:T(8,128)S(1)} %get-tuple-element.66), custom_call_target="InvertDiagBlocksLowerTriangular" | custom-call | tf_op jit(solution)/shard_map/jit(cholesky)/cholesky | solution.py:81
  562.9 11.7 %cholesky.398 = f32[128,128]{1,0:T(8,128)S(1)} custom-call(f32[128,128]{1,0:T(8,128)S(1)} %cholesky.448), custom_call_target="Cholesky" | custom-call | tf_op jit(solution)/shard_map/jit(cholesky)/cholesky | solution.py:81
  575.3 9.8 %custom-call.38 = f32[1,128,128]{1,2,0:T(8,128)S(1)} custom-call(f32[1,128,128]{2,1,0:T(8,128)S(1)} %get-tuple-element.63), custom_call_target="InvertDiagBlocksLowerTriangular" | custom-call | tf_op jit(solution)/shard_map/jit(cholesky)/cholesky | solution.py:81
  586.5 11.7 %cholesky.415 = f32[128,128]{1,0:T(8,128)S(1)} custom-call(f32[128,128]{1,0:T(8,128)S(1)} %convolution_subtract_fusion.15), custom_call_target="Cholesky" | custom-call | tf_op jit(solution)/shard_map/jit(cholesky)/cholesky | solution.py:81
  601.9 8.0 while.5
  609.9 39.3 %custom-call.26 = f32[4,128,128]{1,2,0:T(8,128)S(1)} custom-call(f32[4,128,128]{2,1,0:T(8,128)S(1)} %get-tuple-element.20), custom_call_target="InvertDiagBlocksLowerTriangular" | custom-call | tf_op jit(solution)/shard_map/triangular_solve | solution.py:17
  653.3 113.8 %all-reduce.8.cloned.1.call-done = f32[512,1,256]{2,0,1:T(8,128)} async-done(((f32[512,1,256]{2,0,1:T(8,128)}), f32[512,1,256]{2,0,1:T(8,128)}) %all-reduce.8.cloned.1.call-update) | async-done | bytes 524304 | tf_op jit(solution)/shard_map/psum | solution.py:13
  767.2 2.0 fusion.23
  770.5 20.7 %all-gather.9.cloned.1.call-done = f32[512,2,256]{2,0,1:T(8,128)} async-done(((f32[512,1,256]{2,0,1:T(8,128)}), f32[512,2,256]{2,0,1:T(8,128)}) %all-gather.9.cloned.1.call-update) | async-done | bytes 1048592 | tf_op jit(solution)/shard_map/all_gather | solution.py:84
  (145 shorter events, 73.7 us)
Async XLA Ops:
  7.2 214.4 %all-gather.11.cloned.1.call-start = ((), (), s32[]{:S(2)}) async-start(), calls=%async_computation.7 | async-start | bytes 4210688 | tf_op jit(solution)/shard_map/all_gather | solution.py:50
  8.6 358.9 %all-gather.7.cloned.1.call-start = ((), (), s32[]{:S(2)}) async-start(), calls=%async_computation.2 | async-start | bytes 1114112 | tf_op jit(solution)/shard_map/all_gather | solution.py:60
  10.3 365.5 %all-gather.13.cloned.1.call-start = ((), (), s32[]{:S(2)}) async-start(), calls=%async_computation.8 | async-start | bytes 1114112 | tf_op jit(solution)/shard_map/all_gather | solution.py:49
  11.9 403.3 %reduce-scatter.2.cloned.1.call-start = ((), (), s32[]{:S(2)}) async-start(), calls=%async_computation.3 | async-start | bytes 1572864 | tf_op jit(solution)/shard_map/reduce_scatter | solution.py:73
  231.2 1.0 copy-start.1
  372.4 0.7 copy-start.4
  375.8 7.7 copy-start.5
  375.8 7.7 copy-start.9
  382.9 0.7 copy-start.6
  388.7 26.5 %copy-start.7 = (f32[512,1,1,256]{3,2,1,0:T(1,128)S(1)}, f32[512,1,1,256]{3,2,1,0:T(1,128)}, u32[]{:S(2)}) copy-start(f32[512,1,1,256]{3,2,1,0:T(1,128)} %param.8) | copy-start | bytes 1572868
  391.9 96.3 %all-reduce.6.cloned.1.call-start = ((), (), s32[]{:S(2)}) async-start(), calls=%async_computation.4 | async-start | bytes 524288 | tf_op jit(solution)/shard_map/psum | solution.py:13
  416.4 0.8 copy-start.2
  490.3 22.1 %all-to-all-start = ((f32[512,16,32]{0,2,1:T(8,128)}), f32[512,16,32]{0,2,1:T(8,128)S(1)}, u32[]{:S(2)}, u32[]{:S(2)}) async-start(f32[512,16,32]{0,2,1:T(8,128)} %tile.2), calls=%async_computation.1 | async-start | bytes 2097152 | tf_op jit(solution)/shard_map/all_to_all | solution.py:80
  496.1 271.1 %all-reduce.8.cloned.1.call-start = ((), (), s32[]{:S(2)}) async-start(), calls=%async_computation.5 | async-start | bytes 1048576 | tf_op jit(solution)/shard_map/psum | solution.py:13
  513.0 1.0 copy-start
  649.2 1.5 copy-start.8
  651.1 141.6 %copy-start.3 = (f32[512,256]{1,0:T(8,128)S(1)}, f32[512,256]{1,0:T(8,128)}, u32[]{:S(2)}) copy-start(f32[512,256]{1,0:T(8,128)} %copy-done.2) | copy-start | bytes 1572868
  653.3 137.9 %all-gather.9.cloned.1.call-start = ((), (), s32[]{:S(2)}) async-start(), calls=%async_computation.6 | async-start | bytes 1572864 | tf_op jit(solution)/shard_map/all_gather | solution.py:84
Sparse Core Ops, SparseCore 0:
  13.1 208.4 all-gather.10
  225.1 59.4 all-gather.6
  287.2 63.3 all-gather.12
  392.0 23.1 reduce-scatter.1
  443.4 44.7 all-reduce.5
  653.4 113.7 all-reduce.7
  769.4 21.7 all-gather.8
